TPU v7x, 512 devices: a whole 4x4x16 slice. The times are simulated.
512 devices in a mesh: row: 32 (over x, y, core), col: 16 (over z).
Axes of the slice: x: 4, y: 4, z: 16, core: 2. Of those that a mesh axis runs over, the one named last changes fastest.
Arguments:
- diag_factor: float32 [1024, 1024], P('row', 'col'), may hold values from -1 to 2.5, as said below
- panel_factor: float32 [16384, 1024], P('row', 'col'), may hold values from -0.046875 to 0.046875
- left_factor: float32 [16384, 8192], P('row', 'col'), may hold values from -0.046875 to 0.046875
- pivot_factor: float32 [1024, 8192], P('row', 'col'), may hold values from -0.1875 to 0.1875
- panel_adjoint: float32 [16384, 1024], P('row', 'col'), may hold values from -6 to 6
- left_adjoint: float32 [16384, 8192], P('row', 'col'), may hold values from -6 to 6
- pivot_adjoint: float32 [1024, 8192], P('row', 'col'), may hold values from -6 to 6
- diag_adjoint: float32 [1024, 1024], P('row', 'col'), may hold values from -6 to 6
Outputs:
- solved_panel: float32 [16384, 1024], P('row', 'col')
- left_out: float32 [16384, 8192], P('row', 'col')
- pivot_out: float32 [1024, 8192], P('row', 'col')
- diag_out: float32 [1024, 1024], P('row', 'col')
Inputs may be any that keep to these rules, and one draw needn't show every extreme that they name: diag_factor is lower triangular: zero above the diagonal, diagonal entries at least 1.
All inputs are finite; a program needn't handle non-finite values.
Results may differ from a plain program's by a relative error of at most 0.000073.
Values sent between devices are 32-bit elements; how exact they have to be, the bound alone decides.
A program may use at most 64 MiB of HBM per device.

v0:
```python
import jax
import jax.numpy as jnp
from jax import lax
from jax.sharding import PartitionSpec as P


def right_solve(tile, source):
    return jax.scipy.linalg.solve_triangular(tile, source.T, trans="T", lower=True).T


def local(
    diag_factor,
    panel_factor,
    left_factor,
    pivot_factor,
    panel_adjoint,
    left_adjoint,
    pivot_adjoint,
    diag_adjoint,
):
    highest = lax.Precision.HIGHEST
    block_width = panel_adjoint.shape[1]
    my_col = lax.axis_index("col")
    my_row = lax.axis_index("row")
    column_block = lax.all_gather(diag_factor, "row", axis=0, tiled=True)
    whole_diag = lax.all_gather(column_block, "col", axis=1, tiled=True)
    full_rows = lax.all_gather(panel_adjoint, "col", axis=1, tiled=True)
    solved = right_solve(whole_diag, full_rows)
    solved_panel = lax.dynamic_slice_in_dim(solved, my_col * block_width, block_width, 1)
    picked = solved
    left_out = left_adjoint - jnp.dot(
        picked,
        lax.all_gather(pivot_factor, "row", axis=0, tiled=True),
        precision=highest,
        preferred_element_type=jnp.float32,
    )
    own_rows = diag_adjoint.shape[0]
    picked = solved
    pivot_sum = lax.psum_scatter(
        jnp.einsum("rk,rc->kc", picked, left_factor, precision=highest),
        "row",
        scatter_dimension=0,
        tiled=True,
    )
    picked = solved
    square_sum = lax.psum_scatter(
        jnp.einsum("rk,rc->kc", picked, panel_factor, precision=highest),
        "row",
        scatter_dimension=0,
        tiled=True,
    )
    pivot_out = pivot_adjoint - pivot_sum
    global_row = my_row * own_rows + lax.broadcasted_iota(jnp.int32, (own_rows, block_width), 0)
    global_col = my_col * block_width + lax.broadcasted_iota(jnp.int32, (own_rows, block_width), 1)
    diag_out = diag_adjoint - jnp.where(global_col <= global_row, square_sum, 0.0)
    return (solved_panel, left_out, pivot_out, diag_out)


def solution(mesh):
    in_specs = (
        P("row", "col"),
        P("row", "col"),
        P("row", "col"),
        P("row", "col"),
        P("row", "col"),
        P("row", "col"),
        P("row", "col"),
        P("row", "col"),
    )
    out_specs = (P("row", "col"), P("row", "col"), P("row", "col"), P("row", "col"))
    return jax.shard_map(local, mesh=mesh, in_specs=in_specs, out_specs=out_specs, check_vma=False)
```

profile of v0, /device:TPU:1, one launch (start us, length us, event | category | flops | bytes accessed | tf_op | source)
XLA Modules:
  0.0 463.1 jit_solution(8965409141635587499)
XLA Ops:
  7.2 29.3 %all_gather.12 = f32[1024,64]{1,0:T(8,128)S(1)} all-gather(f32[32,64]{1,0:T(8,128)} %param.8), channel_id=1, replica_groups=mesh['row'=32,'col'=16] {'row'}, dimensions={0}, use_global_device_ids=true | all-gather | bytes 270336 | tf_op jit(solution)/shard_map/all_gather | solution.py:25
  36.5 0.9 copy.14
  37.5 0.7 all-gather.6.cloned.1.call-update
  38.3 0.7 all-gather.8.cloned.1.call-update
  39.0 67.7 %all-gather.4.cloned.1.call-done = f32[1024,1024]{0,1:T(8,128)} async-done(((f32[1024,64]{0,1:T(8,128)}), f32[1024,1024]{0,1:T(8,128)}) %all-gather.4.cloned.1.call-update) | async-done | bytes 4194320 | tf_op jit(solution)/shard_map/all_gather | solution.py:26
  106.7 4.8 %fusion = f32[1024,1024]{0,1:T(8,128)} fusion(f32[1024,1024]{0,1:T(8,128)} %all-gather.4.cloned.1.call-done), kind=kLoop, calls=%fused_computation.3 | loop fusion | flops 2097152 | bytes 8388608 | tf_op jit(solution)/shard_map/jit(_solve_triangular)/triangular_solve | solution.py:8
  111.4 24.1 %while.1 = (s32[]{:T(128)}, f32[1024,1024]{0,1:T(8,128)}, s32[8,2]{0,1:T(2,128)S(1)}, f32[8,128,128]{2,1,0:T(8,128)S(1)}, s32[]{:T(128)}) while((s32[]{:T(128)}, f32[1024,1024]{0,1:T(8,128)}, s32[8,2]{0,1:T(2,128)S(1)}, f32[8,128,128]{2,1,0:T(8,128)S(1)}, s32[]{:T(128)}) %tuple.28), condition=%wide.while_cond, body=%wide.while_body.sunk | while | flops 2 | bytes 393321 | solution.py:8
  111.5 0.5 fusion.55
  112.0 2.3 dynamic-slice.12
  114.5 0.5 fusion.55
  115.1 2.3 dynamic-slice.12
  117.6 0.5 fusion.55
  118.1 2.3 dynamic-slice.12
  120.6 0.5 fusion.55
  121.1 2.3 dynamic-slice.12
  123.6 0.5 fusion.55
  124.1 2.3 dynamic-slice.12
  126.6 0.5 fusion.55
  127.2 2.3 dynamic-slice.12
  129.7 0.5 fusion.55
  130.2 2.3 dynamic-slice.12
  132.7 0.5 fusion.55
  133.2 2.2 dynamic-slice.12
  135.6 78.6 %custom-call.4 = f32[8,128,128]{1,2,0:T(8,128)S(1)} custom-call(f32[8,128,128]{2,1,0:T(8,128)S(1)} %get-tuple-element.11), custom_call_target="InvertDiagBlocksLowerTriangular" | custom-call | tf_op jit(solution)/shard_map/jit(_solve_triangular)/triangular_solve | solution.py:8
  214.2 1.5 fusion.19
  215.7 1.4 convolution_subtract_fusion.4
  217.1 0.4 fusion.25
  217.5 1.4 convolution_subtract_fusion.3
  218.9 0.4 fusion.26
  219.3 1.6 convolution_subtract_fusion.6
  220.9 0.4 fusion.27
  221.2 1.7 convolution_subtract_fusion.7
  222.9 0.4 constant_dynamic-update-slice_fusion.4
  223.4 1.9 convolution_subtract_fusion.2
  225.3 0.4 constant_dynamic-update-slice_fusion.10
  225.8 2.0 convolution_subtract_fusion.5
  227.8 0.4 constant_dynamic-update-slice_fusion.17
  228.4 2.2 convolution_subtract_fusion.1
  230.6 1.2 convolution_dynamic-update-slice_fusion
  232.1 2.6 fusion.36
  235.0 4.8 %fusion.35 = f32[1024,512]{1,0:T(8,128)} fusion(f32[1024,512]{1,0:T(8,128)S(1)} %constant_dynamic-update-slice_fusion.18, f32[512,512]{1,0:T(8,128)S(1)} %copy-done), kind=kOutput, calls=%fused_computation.85 | convolution fusion | flops 3221225472 | bytes 5242880 | tf_op jit(solution)/shard_map/rk,rc->kc/dot_general | solution.py:40
  239.8 0.7 dynamic-slice_bitcast_fusion
  240.5 7.4 %all-gather.8.cloned.1.call-done = f32[1024,512]{1,0:T(8,128)} async-done(((f32[32,512]{1,0:T(8,128)}), f32[1024,512]{1,0:T(8,128)}) %all-gather.8.cloned.1.call-update) | async-done | bytes 2097168 | tf_op jit(solution)/shard_map/all_gather | solution.py:33
  247.9 6.3 %convolution_subtract_fusion = f32[512,512]{1,0:T(8,128)} fusion(f32[512,512]{1,0:T(8,128)} %param.13, f32[1024,512]{1,0:T(8,128)S(1)} %constant_dynamic-update-slice_fusion.18, f32[1024,512]{1,0:T(8,128)} %all-gather.8.cloned.1.call-done), kind=kOutput, calls=%fused_computation.4 | convolution fusion | flops 3221487616 | bytes 6291456 | tf_op jit(solution)/shard_map/dot_general | solution.py:31
  254.2 95.3 %reduce-scatter.5.cloned.1.call-done = f32[32,64]{1,0:T(8,128)} async-done(((f32[1024,64]{1,0:T(8,128)}), f32[32,64]{1,0:T(8,128)}) %reduce-scatter.5.cloned.1.call-update) | async-done | bytes 8208 | tf_op jit(solution)/shard_map/reduce_scatter | solution.py:46
  349.5 1.4 select_subtract_fusion
  350.9 104.3 %reduce-scatter.3.cloned.1.call-done = f32[32,512]{1,0:T(8,128)} async-done(((f32[1024,512]{1,0:T(8,128)}), f32[32,512]{1,0:T(8,128)}) %reduce-scatter.3.cloned.1.call-update) | async-done | bytes 65552 | tf_op jit(solution)/shard_map/reduce_scatter | solution.py:39
  455.1 1.5 sub.10
  (72 shorter events, 2.4 us)
Async XLA Ops:
  7.2 227.8 %copy-start = (f32[512,512]{1,0:T(8,128)S(1)}, f32[512,512]{1,0:T(8,128)}, u32[]{:S(2)}) copy-start(f32[512,512]{1,0:T(8,128)} %param.10) | copy-start | bytes 3145732
  7.2 99.5 %all-gather.4.cloned.1.call-start = ((), (), s32[]{:S(2)}) async-start(), calls=%async_computation.2 | async-start | bytes 4456448 | tf_op jit(solution)/shard_map/all_gather | solution.py:26
  37.5 176.7 %all-gather.6.cloned.1.call-start = ((), (), s32[]{:S(2)}) async-start(), calls=%async_computation.3 | async-start | bytes 2228224 | tf_op jit(solution)/shard_map/all_gather | solution.py:27
  38.2 209.7 %all-gather.8.cloned.1.call-start = ((), (), s32[]{:S(2)}) async-start(), calls=%async_computation.4 | async-start | bytes 2162688 | tf_op jit(solution)/shard_map/all_gather | solution.py:33
  38.9 310.5 %reduce-scatter.5.cloned.1.call-start = ((), (), s32[]{:S(2)}) async-start(), calls=%async_computation.6 | async-start | bytes 540672 | tf_op jit(solution)/shard_map/reduce_scatter | solution.py:46
  214.2 13.7 %copy-start.2 = (f32[8,128,128]{1,2,0:T(8,128)}, f32[8,128,128]{1,2,0:T(8,128)S(1)}, u32[]{:S(2)}) copy-start(f32[8,128,128]{1,2,0:T(8,128)S(1)} %custom-call.4) | copy-start | bytes 1572868
  214.2 5.1 %copy-start.1 = (f32[512,1024]{0,1:T(8,128)S(1)}, f32[512,1024]{0,1:T(8,128)}, u32[]{:S(2)}) copy-start(f32[512,1024]{0,1:T(8,128)} %all-gather.6.cloned.1.call-done) | copy-start | bytes 6291460
  230.6 1.5 copy-start.3
  234.7 220.5 %reduce-scatter.3.cloned.1.call-start = ((), (), s32[]{:S(2)}) async-start(), calls=%async_computation.5 | async-start | bytes 2162688 | tf_op jit(solution)/shard_map/reduce_scatter | solution.py:39
  240.5 109.0 %copy-start.5 = (f32[32,64]{1,0:T(8,128)S(1)}, f32[32,64]{1,0:T(8,128)}, u32[]{:S(2)}) copy-start(f32[32,64]{1,0:T(8,128)} %param.15) | copy-start | bytes 24580
  240.5 214.7 %copy-start.4 = (f32[32,512]{1,0:T(8,128)S(1)}, f32[32,512]{1,0:T(8,128)}, u32[]{:S(2)}) copy-start(f32[32,512]{1,0:T(8,128)} %param.14) | copy-start | bytes 196612
Sparse Core Ops, SparseCore 0:
  37.6 69.0 all-gather.3
  108.7 70.0 all-gather.5
  181.9 65.8 all-gather.7
  252.0 97.3 reduce-scatter.4
  353.7 101.3 reduce-scatter.2
where the time goes:
time: 465 us; the launch traced here: 463 us
  waiting for transfers between devices  276 us (59%)
  other arithmetic  86.2 us (19%)
  matrix products  30.8 us (7%)
  blocking collectives  29.3 us (6%)
  local copies, waits for them, and re-layouts  25.9 us (6%)
  between operations  14.2 us (3%)
    reduce_scatter x1, waiting for transfers between devices, local(): lax.psum_scatter(jnp.einsum('rk,rc->kc', picked, left_factor, precision=h...  104 us
    reduce_scatter x1, waiting for transfers between devices, local(): lax.psum_scatter(jnp.einsum('rk,rc->kc', picked, panel_factor, precision=...  95.3 us
    another operation x3, other arithmetic, right_solve(): jax.scipy.linalg.solve_triangular(tile, source.T, trans='T', lower=True)  83.4 us
    all_gather x1, waiting for transfers between devices, local(): whole_diag = lax.all_gather(column_block, 'col', axis=1, tiled=True)  67.7 us
    all_gather x1, blocking collectives, local(): column_block = lax.all_gather(diag_factor, 'row', axis=0, tiled=True)  29.3 us
    another operation x40, local copies, waits for them, and re-layouts  23.8 us
    another operation x15, matrix products, right_solve(): jax.scipy.linalg.solve_triangular(tile, source.T, trans='T', lower=True)  17.1 us
  transfers between devices with their start and end apart: 5, of which 4 were waited for; matrix products, arithmetic and copies ran while one was open for 30% of the time, Pallas kernels for 0%

commit v1 on v0

v1 whole, which is shorter than its diff:
```python
import functools

import jax
import jax.numpy as jnp
from jax import lax
from jax.experimental import pallas as pl
from jax.experimental.pallas import tpu as pltpu
from jax.sharding import PartitionSpec as P

MESH = pl.DeviceIdType.MESH
F32 = jnp.float32
BF16 = jnp.bfloat16
NZ = 16
PIECES = 4


def dg(a, b, ca, cb):
    return lax.dot_general(a, b, (((ca,), (cb,)), ((), ())), preferred_element_type=F32)


def split(value):
    high = value.astype(BF16)
    return high, (value - high.astype(F32)).astype(BF16)


def mm3(a, b, ca=1, cb=0):
    return dg(a[0], b[0], ca, cb) + dg(a[0], b[1], ca, cb) + dg(a[1], b[0], ca, cb)


def invert_small(blocks, n):
    i = lax.broadcasted_iota(jnp.int32, (n, n), 0)
    j = lax.broadcasted_iota(jnp.int32, (n, n), 1)
    eye = i == j
    inverses = []
    for block in blocks:
        diagonal = jnp.where(eye, block, 0.0)
        by_row = 1.0 / jnp.sum(diagonal, axis=1, keepdims=True)
        by_col = 1.0 / jnp.sum(diagonal, axis=0, keepdims=True)
        pair = ((i // 2) == (j // 2)) & (i > j)
        inverses.append(jnp.where(eye, by_row, 0.0) - jnp.where(pair, block * by_row * by_col, 0.0))
    width = 2
    while width < n:
        mask = ((i // (2 * width)) == (j // (2 * width))) & ((i // width) > (j // width))
        parts = [split(w) for w in inverses]
        inner = [mm3(split(jnp.where(mask, d, 0.0)), w) for d, w in zip(blocks, parts)]
        inverses = [w - mm3(p, split(t)) for w, p, t in zip(inverses, parts, inner)]
        width *= 2
        yield None
    yield inverses


def kernel(
    d_ref, r_ref, at_ref, b_ref, ct_ref,
    xr_ref, xs_ref, ps_ref, ds_ref,
    abuf, dslot, dbuf, rbuf, bbuf, cbuf,
    wh, wl, ah, al, xt, xh, xl, bh, bl, rh, rl,
    own1, sib1, got1, own2, sib2, got2, far1, far2, sum1, sum2, end1, end2,
    lsem, a_s, a_r, dz_s, dz_r, d1_s, d1_r, d2_s, d2_r, d3_s, d3_r,
    r1_s, r1_r, r2_s, r2_r, r3_s, r3_r, c_s, c_r, p1_s, p1_r, p2_s, p2_r,
):
    row = lax.axis_index("row")
    z = lax.axis_index("col")
    c = lax.rem(row, 2)
    y = lax.rem(row // 2, 4)
    x = row // 8

    def x_peer(k):
        return {"row": (lax.rem(x + k, 4) * 4 + y) * 2 + c}

    def y_peer(k):
        return {"row": (x * 4 + lax.rem(y + k, 4)) * 2 + c}

    sibling = {"row": row + 1 - 2 * c}
    z_right = {"col": lax.rem(z + 1, NZ)}
    z_left = {"col": lax.rem(z + NZ - 1, NZ)}

    def remote(src, dst, send, recv, device):
        return pltpu.make_async_remote_copy(
            src_ref=src, dst_ref=dst, send_sem=send, recv_sem=recv, device_id=device, device_id_type=MESH
        )

    local_b = pltpu.make_async_copy(b_ref, bbuf, lsem.at[0])
    local_c = pltpu.make_async_copy(ct_ref, cbuf, lsem.at[1])
    local_a = pltpu.make_async_copy(at_ref, abuf.at[z], lsem.at[2])
    local_r = pltpu.make_async_copy(r_ref, rbuf.at[x, y, c], lsem.at[3])
    local_a.start()
    local_r.start()
    local_b.start()
    local_c.start()

    barrier = pltpu.get_barrier_semaphore()
    greeted = [x_peer(k) for k in (1, 2, 3)] + [y_peer(k) for k in (1, 2, 3)] + [sibling, z_right, z_left]
    for device in greeted:
        pl.semaphore_signal(barrier, inc=1, device_id=device, device_id_type=MESH)
    own_d = d_ref[...]
    dslot[z] = jnp.concatenate([own_d[:16], own_d[16:]], axis=1)
    pl.semaphore_wait(barrier, len(greeted))

    ring_d = {}

    def d_step(s):
        if s > 1:
            for d in range(2):
                ring_d[d, s - 1].wait_recv()
        if s > 8:
            return
        for d in range(2):
            if s == 8 and d == 1:
                continue
            block = lax.rem(z + NZ - (s - 1), NZ) if d == 0 else lax.rem(z + (s - 1), NZ)
            copy = remote(
                dslot.at[block], dslot.at[block], dz_s.at[d, s - 1], dz_r.at[d, s - 1], z_right if d == 0 else z_left
            )
            copy.start()
            ring_d[d, s] = copy

    ring_a = {}
    lanes = 512 // PIECES

    def a_goes(d, s, p):
        return s < 8 or (p < PIECES // 2) == (d == 0)

    def a_piece(s, p):
        if s > 1:
            for d in range(2):
                if a_goes(d, s - 1, p):
                    ring_a[d, s - 1, p].wait_recv()
        if s > 8:
            return
        for d in range(2):
            if not a_goes(d, s, p):
                continue
            block = lax.rem(z + NZ - (s - 1), NZ) if d == 0 else lax.rem(z + (s - 1), NZ)
            cut = pl.ds(p * lanes, lanes)
            src = (at_ref if s == 1 else abuf.at[block]).at[:, cut]
            copy = remote(
                src, abuf.at[block].at[:, cut], a_s.at[d, s - 1, p], a_r.at[d, s - 1, p],
                z_right if d == 0 else z_left,
            )
            copy.start()
            ring_a[d, s, p] = copy

    def a_split(block):
        value = abuf[block]
        high, low = split(value)
        ah[block] = high
        al[block] = low

    a_queue = [(s, p) for s in range(1, 9) for p in range(PIECES)]

    def a_pump(count=PIECES):
        for _ in range(count):
            if not a_queue:
                return
            s, p = a_queue.pop(0)
            a_piece(s, p)
            if p == PIECES - 1 and s > 1:
                a_split(lax.rem(z + NZ - (s - 1), NZ))
                a_split(lax.rem(z + (s - 1), NZ))

    def r_cut(px, py, half):
        return rbuf.at[px, py, c, :, pl.ds(half * 256, 256)]

    r_copies = []
    d_step(1)
    for k in (2, 1, 3):
        for half, peer in ((0, x_peer(k)), (1, y_peer(k))):
            copy = remote(
                r_ref.at[:, pl.ds(half * 256, 256)], r_cut(x, y, half), r1_s.at[half, k - 1], r1_r.at[half, k - 1], peer
            )
            copy.start()
            r_copies.append(copy)
    a_pump()
    d_step(2)
    d_step(3)
    for copy in r_copies:
        copy.wait()
    local_r.wait()
    r_far = []
    for k in (2, 1, 3):
        half0 = rbuf.at[:, y, c, :, pl.ds(0, 256)]
        half1 = rbuf.at[x, :, c, :, pl.ds(256, 256)]
        for half, cut, peer in ((0, half0, y_peer(k)), (1, half1, x_peer(k))):
            copy = remote(cut, cut, r2_s.at[half, k - 1], r2_r.at[half, k - 1], peer)
            copy.start()
            r_far.append(copy)
    d_step(4)
    local_a.wait()
    a_split(z)
    a_pump()
    d_step(5)
    d_step(6)
    d_step(7)
    a_pump()
    d_step(8)
    ring_d[0, 8].wait_recv()

    for q in range(8):
        first = dslot[2 * q]
        second = dslot[2 * q + 1]
        dbuf[x, y, c, 0:16, q * 128:(q + 1) * 128] = jnp.concatenate([first[:, :64], second[:, :64]], axis=1)
        dbuf[x, y, c, 16:32, q * 128:(q + 1) * 128] = jnp.concatenate([first[:, 64:], second[:, 64:]], axis=1)

    def when(condition, action):
        if condition is None:
            action()
        else:
            pl.when(condition)(action)

    def at_least(value, q):
        return None if q == 0 else value >= q

    x_first = (0, 3)
    d_near = {}
    for q in range(4):
        cut = dbuf.at[x, y, c, :, pl.ds(q * 256, 256)]
        for k in (2, 1, 3):
            peer = x_peer(k) if q in x_first else y_peer(k)
            d_near[q, k] = remote(cut, cut, d1_s.at[q, k - 1], d1_r.at[q, k - 1], peer)
            when(at_least(x, q), d_near[q, k].start)
    a_pump()
    d_far = {}
    for q in range(4):
        for k in (2, 1, 3):
            if q in x_first:
                when(at_least(lax.rem(x + 4 - k, 4), q), d_near[q, k].wait_recv)
            else:
                when(at_least(x, q), d_near[q, k].wait_recv)
        for k in (2, 1, 3):
            if q in x_first:
                cut = dbuf.at[pl.ds(q, 4 - q), y, c, :, pl.ds(q * 256, 256)]
                d_far[q, k] = remote(cut, cut, d2_s.at[q, k - 1], d2_r.at[q, k - 1], y_peer(k))
                d_far[q, k].start()
            else:
                cut = dbuf.at[x, :, c, :, pl.ds(q * 256, 256)]
                d_far[q, k] = remote(cut, cut, d2_s.at[q, k - 1], d2_r.at[q, k - 1], x_peer(k))
                when(at_least(x, q), d_far[q, k].start)
    local_b.wait()
    high, low = split(bbuf[...])
    bh[...] = high
    bl[...] = low
    local_c.wait()
    c_parts = split(cbuf[...])
    a_pump()
    for copy in r_far:
        copy.wait()
    r_pair = remote(rbuf.at[:, :, c], rbuf.at[:, :, c], r3_s, r3_r, sibling)
    r_pair.start()
    d_pair = []
    for q in range(4):
        for k in (2, 1, 3):
            if q in x_first:
                d_far[q, k].wait_recv()
            else:
                when(at_least(lax.rem(x + 4 - k, 4), q), d_far[q, k].wait_recv)
        cut = dbuf.at[pl.ds(q, 4 - q), :, c, :, pl.ds(q * 256, 256)]
        copy = remote(cut, cut, d3_s.at[q], d3_r.at[q], sibling)
        copy.start()
        d_pair.append(copy)
    a_pump()
    for copy in d_pair:
        copy.wait()

    def d_block(i, j, size):
        per = size // 64
        value = dbuf[:] if False else None
        del value
        rows = []
        first = i * size
        x0, y0 = first // 256, (first % 256) // 64
        if size >= 256:
            for step in range(size // 256):
                rows.append(dbuf[x0 + step, :, :, :, j * size:(j + 1) * size].reshape(256, size))
            return rows[0] if len(rows) == 1 else jnp.concatenate(rows, axis=0)
        return dbuf[x0, y0:y0 + per, :, :, j * size:(j + 1) * size].reshape(size, size)

    def w_get(i, j, size):
        cut = (slice(i * size, (i + 1) * size), slice(j * size, (j + 1) * size))
        return wh[cut], wl[cut]

    def w_put(i, j, size, value):
        high, low = split(value)
        wh[i * size:(i + 1) * size, j * size:(j + 1) * size] = high
        wl[i * size:(i + 1) * size, j * size:(j + 1) * size] = low

    result = None
    for level, result in enumerate(invert_small([d_block(k, k, 128) for k in range(8)], 128)):
        if level % 2 == 1:
            a_pump(2)
    for k in range(8):
        w_put(k, k, 128, result[k])
        if k % 2 == 0:
            wh[k * 128:(k + 1) * 128, (k + 1) * 128:(k + 2) * 128] = jnp.zeros((128, 128), BF16)
            wl[k * 128:(k + 1) * 128, (k + 1) * 128:(k + 2) * 128] = jnp.zeros((128, 128), BF16)
    for size in (128, 256, 512):
        pairs = range(0, 1024 // size, 2)
        inner = [mm3(split(d_block(k + 1, k, size)), w_get(k, k, size)) for k in pairs]
        for k, value in zip(pairs, inner):
            w_put(k + 1, k, size, -mm3(w_get(k + 1, k + 1, size), split(value)))
            if size == 256:
                wh[k * size:(k + 1) * size, (k + 1) * size:(k + 2) * size] = jnp.zeros((size, size), BF16)
                wl[k * size:(k + 1) * size, (k + 1) * size:(k + 2) * size] = jnp.zeros((size, size), BF16)
        a_pump(2)
    while a_queue:
        a_pump(1)
    r_pair.wait()
    high, low = split(rbuf[...].reshape(1024, 512))
    rh[...] = high
    rl[...] = low
    for p in range(PIECES):
        a_piece(9, p)
    a_split(lax.rem(z + 8, NZ))

    for jb in range(4):
        k0 = jb * 256
        w_parts = (wh[k0:, k0:k0 + 256], wl[k0:, k0:k0 + 256])
        a_parts = (ah[4 * jb:].reshape(1024 - k0, 512), al[4 * jb:].reshape(1024 - k0, 512))
        value = mm3(w_parts, a_parts, 0, 0)
        high, low = split(value)
        xt[4 * jb:4 * jb + 4] = value.reshape(4, 64, 512)
        xh[4 * jb:4 * jb + 4] = high.reshape(4, 64, 512)
        xl[4 * jb:4 * jb + 4] = low.reshape(4, 64, 512)

    pair_copies = {}

    def start_task(half, k):
        if half == 0:
            first = 4 * lax.rem(x + k, 4)
            x_parts = (xh[pl.ds(first, 4)].reshape(256, 512), xl[pl.ds(first, 4)].reshape(256, 512))
        else:
            other = lax.rem(y + k, 4)
            x_parts = tuple(jnp.concatenate([ref[4 * g + other] for g in range(4)], axis=0) for ref in (xh, xl))
        cut = slice(half * 256, half * 256 + 256)
        value = mm3(x_parts, (bh[:, cut], bl[:, cut])).reshape(4, 2, 32, 256)
        own, sib, got = ((own1, sib1, got1), (own2, sib2, got2))[half]
        first_core, second_core = value[:, 0], value[:, 1]
        own[k, :, 0:32] = jnp.where(c == 0, first_core, second_core)
        sib[k, :, 0:32] = jnp.where(c == 0, second_core, first_core)
        if half == 0:
            square = mm3(x_parts, c_parts, 1, 1).reshape(4, 2, 4, 8, 64)
            packed = jnp.concatenate([square[:, :, g] for g in range(4)], axis=-1)
            own[k, :, 32:40] = jnp.where(c == 0, packed[:, 0], packed[:, 1])
            sib[k, :, 32:40] = jnp.where(c == 0, packed[:, 1], packed[:, 0])
        copy = remote(sib.at[k], got.at[k], c_s.at[half, k], c_r.at[half, k], sibling)
        copy.start()
        pair_copies[half, k] = copy

    far_copies = {}

    def finish_task(half, k):
        own, _, got = ((own1, sib1, got1), (own2, sib2, got2))[half]
        far = (far1, far2)[half]
        pair_copies[half, k].wait_recv()
        own[k] = own[k] + got[k]
        if k:
            peer = x_peer(k) if half == 0 else y_peer(k)
            copy = remote(own.at[k], far.at[k - 1], p1_s.at[half, k - 1], p1_r.at[half, k - 1], peer)
            copy.start()
            far_copies[half, k] = copy

    tasks = [(half, k) for k in (2, 1, 3, 0) for half in (0, 1)]
    for position, task in enumerate(tasks):
        start_task(*task)
        if position >= 2:
            finish_task(*tasks[position - 2])
    finish_task(*tasks[-2])
    finish_task(*tasks[-1])

    def xr_part(g):
        cut = slice(g * 256, g * 256 + 256)
        x_parts = (xh[...].reshape(1024, 512)[:, cut], xl[...].reshape(1024, 512)[:, cut])
        xr_ref[cut, :] = mm3(x_parts, (rh[...], rl[...]), 0, 0)

    xr_part(0)
    end_copies = {}
    for half in range(2):
        own, far, total = ((own1, far1, sum1), (own2, far2, sum2))[half]
        end = (end1, end2)[half]
        for k in (1, 2, 3):
            far_copies[half, k].wait_recv()
        total[...] = own[0] + far[0] + far[1] + far[2]
        for k in (2, 1, 3):
            place = lax.rem((y if half == 0 else x) + k, 4)
            peer = y_peer(k) if half == 0 else x_peer(k)
            copy = remote(total.at[place], end.at[k - 1], p2_s.at[half, k - 1], p2_r.at[half, k - 1], peer)
            copy.start()
            end_copies[half, k] = copy
    xr_part(1)
    xs_ref[...] = xt[z]
    for half in range(2):
        total = (sum1, sum2)[half]
        end = (end1, end2)[half]
        for k in (1, 2, 3):
            end_copies[half, k].wait_recv()
        value = total[y if half == 0 else x] + end[0] + end[1] + end[2]
        ps_ref[:, half * 256:half * 256 + 256] = value[:32]
        if half == 0:
            for g in range(4):
                ds_ref[8 * g:8 * g + 8, :] = value[32:40, 64 * g:64 * g + 64]

    for copy in ring_d.values():
        copy.wait_send()
    for copy in ring_a.values():
        copy.wait_send()
    for q in range(4):
        for k in (1, 2, 3):
            when(at_least(x, q), d_near[q, k].wait_send)
            if q in x_first:
                d_far[q, k].wait_send()
            else:
                when(at_least(x, q), d_far[q, k].wait_send)
    for group in (pair_copies, far_copies, end_copies):
        for copy in group.values():
            copy.wait_send()


def fused(d, r, at, b, ct):
    dma = pltpu.SemaphoreType.DMA
    vmem = pltpu.VMEM
    any_space = pl.BlockSpec(memory_space=pl.ANY)
    in_vmem = pl.BlockSpec(memory_space=pltpu.VMEM)
    return pl.pallas_call(
        kernel,
        out_shape=(
            jax.ShapeDtypeStruct((512, 512), F32),
            jax.ShapeDtypeStruct((64, 512), F32),
            jax.ShapeDtypeStruct((32, 512), F32),
            jax.ShapeDtypeStruct((32, 64), F32),
        ),
        in_specs=[in_vmem, any_space, any_space, any_space, any_space],
        out_specs=(in_vmem,) * 4,
        scratch_shapes=[
            vmem((16, 64, 512), F32),
            vmem((16, 16, 128), F32),
            vmem((4, 4, 2, 32, 1024), F32),
            vmem((4, 4, 2, 32, 512), F32),
            vmem((512, 512), F32),
            vmem((64, 512), F32),
            vmem((1024, 1024), BF16),
            vmem((1024, 1024), BF16),
            vmem((16, 64, 512), BF16),
            vmem((16, 64, 512), BF16),
            vmem((16, 64, 512), F32),
            vmem((16, 64, 512), BF16),
            vmem((16, 64, 512), BF16),
            vmem((512, 512), BF16),
            vmem((512, 512), BF16),
            vmem((1024, 512), BF16),
            vmem((1024, 512), BF16),
            vmem((4, 4, 40, 256), F32),
            vmem((4, 4, 40, 256), F32),
            vmem((4, 4, 40, 256), F32),
            vmem((4, 4, 32, 256), F32),
            vmem((4, 4, 32, 256), F32),
            vmem((4, 4, 32, 256), F32),
            vmem((3, 4, 40, 256), F32),
            vmem((3, 4, 32, 256), F32),
            vmem((4, 40, 256), F32),
            vmem((4, 32, 256), F32),
            vmem((3, 40, 256), F32),
            vmem((3, 32, 256), F32),
            dma((4,)),
            dma((2, 8, PIECES)), dma((2, 8, PIECES)),
            dma((2, 8)), dma((2, 8)),
            dma((4, 3)), dma((4, 3)),
            dma((4, 3)), dma((4, 3)),
            dma((4,)), dma((4,)),
            dma((2, 3)), dma((2, 3)),
            dma((2, 3)), dma((2, 3)),
            dma, dma,
            dma((2, 4)), dma((2, 4)),
            dma((2, 3)), dma((2, 3)),
            dma((2, 3)), dma((2, 3)),
        ],
        compiler_params=pltpu.CompilerParams(
            collective_id=0, has_side_effects=True, vmem_limit_bytes=56 * 1024 * 1024
        ),
        cost_estimate=pl.CostEstimate(flops=6 * 10**9, bytes_accessed=8 * 2**20, transcendentals=0),
    )(d, r, at, b, ct)


def local(
    diag_factor,
    panel_factor,
    left_factor,
    pivot_factor,
    panel_adjoint,
    left_adjoint,
    pivot_adjoint,
    diag_adjoint,
):
    rows, width = diag_adjoint.shape
    xr, solved, pivot_sum, square_sum = fused(
        diag_factor, pivot_factor, panel_adjoint.T, left_factor, panel_factor.T
    )
    global_row = lax.axis_index("row") * rows + lax.broadcasted_iota(jnp.int32, (rows, width), 0)
    global_col = lax.axis_index("col") * width + lax.broadcasted_iota(jnp.int32, (rows, width), 1)
    left_out = left_adjoint - xr
    pivot_out = pivot_adjoint - pivot_sum
    diag_out = diag_adjoint - jnp.where(global_col <= global_row, square_sum, 0.0)
    return (solved.T, left_out, pivot_out, diag_out)


def solution(mesh):
    spec = P("row", "col")
    return jax.shard_map(
        local, mesh=mesh, in_specs=(spec,) * 8, out_specs=(spec,) * 4, check_vma=False
    )
```

time: 465 us -> 94.2 us (0.20)
  waiting for transfers between devices: 276 us -> 0 us
  Pallas kernels: 0 us -> 87.2 us
  other arithmetic: 86.2 us -> 5.32 us
  matrix products: 30.8 us -> 0 us
  blocking collectives: 29.3 us -> 0 us
  local copies, waits for them, and re-layouts: 25.9 us -> 0.68 us
  between operations: 14.2 us -> 0.69 us
    reduce_scatter x2 -> x0, waiting for transfers between devices: 200 us -> none  [the longest x1 104 us: local(): lax.psum_scatter(jnp.einsum('rk,rc->kc', picked, left_factor, precision=h...]
    pallas_call x0 -> x1, Pallas kernels: none -> 87.2 us  [fused(): pl.pallas_call(kernel, out_shape=(jax.ShapeDtypeStruct((512, 512), F32),...]
    another operation x3 -> x0, other arithmetic: 83.4 us -> none  [right_solve(): jax.scipy.linalg.solve_triangular(tile, source.T, trans='T', lower=True)]
    all_gather x3 -> x0, waiting for transfers between devices: 75.1 us -> none  [the longest x1 67.7 us: local(): whole_diag = lax.all_gather(column_block, 'col', axis=1, tiled=True)]
    all_gather x1 -> x0, blocking collectives: 29.3 us -> none  [local(): column_block = lax.all_gather(diag_factor, 'row', axis=0, tiled=True)]
    another operation x45 -> x0, local copies, waits for them, and re-layouts: 23.9 us -> none
    another operation x15 -> x0, matrix products: 17.1 us -> none  [right_solve(): jax.scipy.linalg.solve_triangular(tile, source.T, trans='T', lower=True)]
    dot_general x3 -> x0, matrix products: 13.7 us -> none  [the longest x1 6.32 us: local(): jnp.dot(picked, lax.all_gather(pivot_factor, 'row', axis=0, tiled=True),...]
  transfers between devices with their start and end apart: 5 -> 0, of which waited for: 4 -> 0; matrix products, arithmetic and copies ran while one was open for 30% -> 0% of each run, Pallas kernels for 0% -> 0%
where the time goes in v1:
time: 94.2 us; the launch traced here: 93.9 us
  Pallas kernels  87.2 us (93%)
  other arithmetic  5.32 us (6%)
    pallas_call x1, Pallas kernels, fused(): pl.pallas_call(kernel, out_shape=(jax.ShapeDtypeStruct((512, 512), F32),...  87.2 us
    sub x1, other arithmetic, local(): left_out = left_adjoint - xr  2.44 us

profile of v1, /device:TPU:1, one launch (start us, length us, event | category | flops | bytes accessed | tf_op | source)
XLA Modules:
  0.0 93.9 jit_solution(10981787337926057007)
XLA Ops:
  0.7 0.0 copy-start.3
  0.7 0.0 copy-start.2
  0.7 0.0 copy-start
  0.7 87.2 %shard_map.111 = (f32[512,512]{1,0:T(8,128)}, f32[64,512]{1,0:T(8,128)}, f32[32,512]{1,0:T(8,128)}, f32[32,64]{1,0:T(8,128)}) custom-call(f32[32,64]{1,0:T(8,128)} %d_ref.1, f32[32,512]{1,0:T(8,128)} %r_ref.1, f32[64,512]{1,0:T(8,128)} %bitcast.4, f32[512,512]{1,0:T(8,128)} %b_ref.1, f32[64,512]{1,0:T(8,128)} %bitcast.5), custom_call_target="tpu_custom_call" | custom-call | flops 6000000000 | bytes 8388608 | tf_op jit(solution)/shard_map/pallas_call | solution.py:422
  87.9 0.0 copy-done.3
  87.9 1.4 %select_subtract_fusion = f32[32,64]{1,0:T(8,128)} fusion(f32[32,64]{1,0:T(8,128)S(1)} %copy-done.3, f32[32,64]{1,0:T(8,128)} %get-tuple-element.11, s32[64]{0:T(128)S(1)} %iota_add_fusion.1, s32[32]{0:T(128)S(1)} %iota_add_fusion), kind=kLoop, calls=%fused_computation | loop fusion | flops 6144 | bytes 24960 | tf_op jit(solution)/shard_map/sub | solution.py:500
  89.3 0.0 copy-done.2
  89.3 1.5 %sub.10 = f32[32,512]{1,0:T(8,128)} subtract(f32[32,512]{1,0:T(8,128)S(1)} %copy-done.2, f32[32,512]{1,0:T(8,128)} %get-tuple-element.10) | non-fusion elementwise | flops 16384 | bytes 196608 | tf_op jit(solution)/shard_map/sub | solution.py:499
  90.8 0.0 copy-done
  90.8 0.0 copy-start.1
  90.8 2.4 %sub.9 = f32[512,512]{1,0:T(8,128)} subtract(f32[512,512]{1,0:T(8,128)S(1)} %copy-done, f32[512,512]{1,0:T(8,128)} %get-tuple-element.9) | non-fusion elementwise | flops 262144 | bytes 3145728 | tf_op jit(solution)/shard_map/sub | solution.py:498
  93.3 0.0 copy-done.1
  93.3 0.7 copy.13
  (2 shorter events, 0.0 us)
Async XLA Ops:
  0.7 87.3 %copy-start.3 = (f32[32,64]{1,0:T(8,128)S(1)}, f32[32,64]{1,0:T(8,128)}, u32[]{:S(2)}) copy-start(f32[32,64]{1,0:T(8,128)} %param.15) | copy-start | bytes 24580
  0.7 88.7 %copy-start.2 = (f32[32,512]{1,0:T(8,128)S(1)}, f32[32,512]{1,0:T(8,128)}, u32[]{:S(2)}) copy-start(f32[32,512]{1,0:T(8,128)} %param.14) | copy-start | bytes 196612
  0.7 90.1 %copy-start = (f32[512,512]{1,0:T(8,128)S(1)}, f32[512,512]{1,0:T(8,128)}, u32[]{:S(2)}) copy-start(f32[512,512]{1,0:T(8,128)} %param.13) | copy-start | bytes 3145732
  90.8 2.4 %copy-start.1 = (f32[64,512]{1,0:T(8,128)S(1)}, f32[64,512]{1,0:T(8,128)}, u32[]{:S(2)}) copy-start(f32[64,512]{1,0:T(8,128)} %get-tuple-element.8) | copy-start | bytes 393220

commit v2 on v1

--- a/solution.py
+++ b/solution.py
@@ -54,7 +54,7 @@
     xr_ref, xs_ref, ps_ref, ds_ref,
     abuf, dslot, dbuf, rbuf, bbuf, cbuf,
     wh, wl, ah, al, xt, xh, xl, bh, bl, rh, rl,
-    own1, sib1, got1, own2, sib2, got2, far1, far2, sum1, sum2, end1, end2,
+    xrbuf, own1, sib1, got1, own2, sib2, got2, far1, far2, sum1, sum2, end1, end2,
     lsem, a_s, a_r, dz_s, dz_r, d1_s, d1_r, d2_s, d2_r, d3_s, d3_r,
     r1_s, r1_r, r2_s, r2_r, r3_s, r3_r, c_s, c_r, p1_s, p1_r, p2_s, p2_r,
 ):
@@ -71,8 +71,11 @@
         return {"row": (x * 4 + lax.rem(y + k, 4)) * 2 + c}
 
     sibling = {"row": row + 1 - 2 * c}
-    z_right = {"col": lax.rem(z + 1, NZ)}
-    z_left = {"col": lax.rem(z + NZ - 1, NZ)}
+
+    def z_peer(k):
+        return {"col": lax.rem(z + k + NZ, NZ)}
+
+    z_right, z_left = z_peer(1), z_peer(-1)
 
     def remote(src, dst, send, recv, device):
         return pltpu.make_async_remote_copy(
@@ -89,30 +92,29 @@
     local_c.start()
 
     barrier = pltpu.get_barrier_semaphore()
-    greeted = [x_peer(k) for k in (1, 2, 3)] + [y_peer(k) for k in (1, 2, 3)] + [sibling, z_right, z_left]
+    greeted = [x_peer(k) for k in (1, 2, 3)] + [y_peer(k) for k in (1, 2, 3)] + [sibling]
+    greeted += [z_peer(k) for k in (8, 4, -4, 2, -2, 1, -1)]
     for device in greeted:
         pl.semaphore_signal(barrier, inc=1, device_id=device, device_id_type=MESH)
     own_d = d_ref[...]
-    dslot[z] = jnp.concatenate([own_d[:16], own_d[16:]], axis=1)
+    dslot[lax.rem(z, 4), z // 4] = jnp.concatenate([own_d[:16], own_d[16:]], axis=1)
     pl.semaphore_wait(barrier, len(greeted))
 
-    ring_d = {}
-
-    def d_step(s):
-        if s > 1:
-            for d in range(2):
-                ring_d[d, s - 1].wait_recv()
-        if s > 8:
-            return
-        for d in range(2):
-            if s == 8 and d == 1:
-                continue
-            block = lax.rem(z + NZ - (s - 1), NZ) if d == 0 else lax.rem(z + (s - 1), NZ)
-            copy = remote(
-                dslot.at[block], dslot.at[block], dz_s.at[d, s - 1], dz_r.at[d, s - 1], z_right if d == 0 else z_left
-            )
-            copy.start()
-            ring_d[d, s] = copy
+    d_z = {}
+
+    def d_fours():
+        cut = dslot.at[lax.rem(z, 4), z // 4]
+        for i, k in enumerate((8, 4, -4)):
+            d_z[i] = remote(cut, cut, dz_s.at[i], dz_r.at[i], z_peer(k))
+            d_z[i].start()
+
+    def d_near_z():
+        for i in range(3):
+            d_z[i].wait_recv()
+        cut = dslot.at[lax.rem(z, 4)]
+        for i, k in ((3, 2), (4, 1), (5, -1)):
+            d_z[i] = remote(cut, cut, dz_s.at[i], dz_r.at[i], z_peer(k))
+            d_z[i].start()
 
     ring_a = {}
     lanes = 512 // PIECES
@@ -162,7 +164,7 @@
         return rbuf.at[px, py, c, :, pl.ds(half * 256, 256)]
 
     r_copies = []
-    d_step(1)
+    d_fours()
     for k in (2, 1, 3):
         for half, peer in ((0, x_peer(k)), (1, y_peer(k))):
             copy = remote(
@@ -171,8 +173,6 @@
             copy.start()
             r_copies.append(copy)
     a_pump()
-    d_step(2)
-    d_step(3)
     for copy in r_copies:
         copy.wait()
     local_r.wait()
@@ -184,20 +184,15 @@
             copy = remote(cut, cut, r2_s.at[half, k - 1], r2_r.at[half, k - 1], peer)
             copy.start()
             r_far.append(copy)
-    d_step(4)
-    local_a.wait()
-    a_split(z)
-    a_pump()
-    d_step(5)
-    d_step(6)
-    d_step(7)
-    a_pump()
-    d_step(8)
-    ring_d[0, 8].wait_recv()
+    a_pump()
+    d_near_z()
+    a_pump()
+    for i in (3, 4, 5):
+        d_z[i].wait_recv()
 
     for q in range(8):
-        first = dslot[2 * q]
-        second = dslot[2 * q + 1]
+        first = dslot[(2 * q) % 4, q // 2]
+        second = dslot[(2 * q + 1) % 4, q // 2]
         dbuf[x, y, c, 0:16, q * 128:(q + 1) * 128] = jnp.concatenate([first[:, :64], second[:, :64]], axis=1)
         dbuf[x, y, c, 16:32, q * 128:(q + 1) * 128] = jnp.concatenate([first[:, 64:], second[:, 64:]], axis=1)
 
@@ -210,7 +205,7 @@
     def at_least(value, q):
         return None if q == 0 else value >= q
 
-    x_first = (0, 3)
+    x_first = (0, 2, 3)
     d_near = {}
     for q in range(4):
         cut = dbuf.at[x, y, c, :, pl.ds(q * 256, 256)]
@@ -235,6 +230,9 @@
                 cut = dbuf.at[x, :, c, :, pl.ds(q * 256, 256)]
                 d_far[q, k] = remote(cut, cut, d2_s.at[q, k - 1], d2_r.at[q, k - 1], x_peer(k))
                 when(at_least(x, q), d_far[q, k].start)
+    a_pump()
+    local_a.wait()
+    a_split(z)
     local_b.wait()
     high, low = split(bbuf[...])
     bh[...] = high
@@ -242,10 +240,6 @@
     local_c.wait()
     c_parts = split(cbuf[...])
     a_pump()
-    for copy in r_far:
-        copy.wait()
-    r_pair = remote(rbuf.at[:, :, c], rbuf.at[:, :, c], r3_s, r3_r, sibling)
-    r_pair.start()
     d_pair = []
     for q in range(4):
         for k in (2, 1, 3):
@@ -263,8 +257,6 @@
 
     def d_block(i, j, size):
         per = size // 64
-        value = dbuf[:] if False else None
-        del value
         rows = []
         first = i * size
         x0, y0 = first // 256, (first % 256) // 64
@@ -303,10 +295,10 @@
         a_pump(2)
     while a_queue:
         a_pump(1)
-    r_pair.wait()
-    high, low = split(rbuf[...].reshape(1024, 512))
-    rh[...] = high
-    rl[...] = low
+    for copy in r_far:
+        copy.wait()
+    r_pair = remote(rbuf.at[:, :, c], rbuf.at[:, :, c], r3_s, r3_r, sibling)
+    r_pair.start()
     for p in range(PIECES):
         a_piece(9, p)
     a_split(lax.rem(z + 8, NZ))
@@ -354,9 +346,13 @@
         own[k] = own[k] + got[k]
         if k:
             peer = x_peer(k) if half == 0 else y_peer(k)
-            copy = remote(own.at[k], far.at[k - 1], p1_s.at[half, k - 1], p1_r.at[half, k - 1], peer)
-            copy.start()
-            far_copies[half, k] = copy
+            for m in (2, 1, 3, 0):
+                place = lax.rem((y if half == 0 else x) + m, 4)
+                copy = remote(
+                    own.at[k, place], far.at[k - 1, place], p1_s.at[half, k - 1, m], p1_r.at[half, k - 1, m], peer
+                )
+                copy.start()
+                far_copies[half, k, m] = copy
 
     tasks = [(half, k) for k in (2, 1, 3, 0) for half in (0, 1)]
     for position, task in enumerate(tasks):
@@ -369,24 +365,34 @@
     def xr_part(g):
         cut = slice(g * 256, g * 256 + 256)
         x_parts = (xh[...].reshape(1024, 512)[:, cut], xl[...].reshape(1024, 512)[:, cut])
-        xr_ref[cut, :] = mm3(x_parts, (rh[...], rl[...]), 0, 0)
-
+        xrbuf[cut, :] = mm3(x_parts, (rh[...], rl[...]), 0, 0)
+        copy = pltpu.make_async_copy(xrbuf.at[pl.ds(g * 256, 256)], xr_ref.at[pl.ds(g * 256, 256)], lsem.at[4 + g])
+        copy.start()
+        out_copies.append(copy)
+
+    out_copies = [pltpu.make_async_copy(xt.at[z], xs_ref, lsem.at[6])]
+    out_copies[0].start()
+
+    r_pair.wait()
+    high, low = split(rbuf[...].reshape(1024, 512))
+    rh[...] = high
+    rl[...] = low
     xr_part(0)
+    xr_part(1)
     end_copies = {}
-    for half in range(2):
-        own, far, total = ((own1, far1, sum1), (own2, far2, sum2))[half]
-        end = (end1, end2)[half]
-        for k in (1, 2, 3):
-            far_copies[half, k].wait_recv()
-        total[...] = own[0] + far[0] + far[1] + far[2]
-        for k in (2, 1, 3):
-            place = lax.rem((y if half == 0 else x) + k, 4)
-            peer = y_peer(k) if half == 0 else x_peer(k)
-            copy = remote(total.at[place], end.at[k - 1], p2_s.at[half, k - 1], p2_r.at[half, k - 1], peer)
-            copy.start()
-            end_copies[half, k] = copy
-    xr_part(1)
-    xs_ref[...] = xt[z]
+    for m in (2, 1, 3, 0):
+        for half in range(2):
+            own, far, total = ((own1, far1, sum1), (own2, far2, sum2))[half]
+            end = (end1, end2)[half]
+            place = lax.rem((y if half == 0 else x) + m, 4)
+            for k in (1, 2, 3):
+                far_copies[half, k, m].wait_recv()
+            total[place] = own[0, place] + far[0, place] + far[1, place] + far[2, place]
+            if m:
+                peer = y_peer(m) if half == 0 else x_peer(m)
+                copy = remote(total.at[place], end.at[m - 1], p2_s.at[half, m - 1], p2_r.at[half, m - 1], peer)
+                copy.start()
+                end_copies[half, m] = copy
     for half in range(2):
         total = (sum1, sum2)[half]
         end = (end1, end2)[half]
@@ -396,9 +402,14 @@
         ps_ref[:, half * 256:half * 256 + 256] = value[:32]
         if half == 0:
             for g in range(4):
-                ds_ref[8 * g:8 * g + 8, :] = value[32:40, 64 * g:64 * g + 64]
-
-    for copy in ring_d.values():
+                at_row = row * 32 + 8 * g + lax.broadcasted_iota(jnp.int32, (8, 64), 0)
+                at_col = z * 64 + lax.broadcasted_iota(jnp.int32, (8, 64), 1)
+                part = value[32:40, 64 * g:64 * g + 64]
+                ds_ref[8 * g:8 * g + 8, :] = jnp.where(at_col <= at_row, part, 0.0)
+
+    for copy in out_copies:
+        copy.wait()
+    for copy in d_z.values():
         copy.wait_send()
     for copy in ring_a.values():
         copy.wait_send()
@@ -428,10 +439,10 @@
             jax.ShapeDtypeStruct((32, 64), F32),
         ),
         in_specs=[in_vmem, any_space, any_space, any_space, any_space],
-        out_specs=(in_vmem,) * 4,
+        out_specs=(any_space, any_space, in_vmem, in_vmem),
         scratch_shapes=[
             vmem((16, 64, 512), F32),
-            vmem((16, 16, 128), F32),
+            vmem((4, 4, 16, 128), F32),
             vmem((4, 4, 2, 32, 1024), F32),
             vmem((4, 4, 2, 32, 512), F32),
             vmem((512, 512), F32),
@@ -447,6 +458,7 @@
             vmem((512, 512), BF16),
             vmem((1024, 512), BF16),
             vmem((1024, 512), BF16),
+            vmem((512, 512), F32),
             vmem((4, 4, 40, 256), F32),
             vmem((4, 4, 40, 256), F32),
             vmem((4, 4, 40, 256), F32),
@@ -459,9 +471,9 @@
             vmem((4, 32, 256), F32),
             vmem((3, 40, 256), F32),
             vmem((3, 32, 256), F32),
-            dma((4,)),
+            dma((7,)),
             dma((2, 8, PIECES)), dma((2, 8, PIECES)),
-            dma((2, 8)), dma((2, 8)),
+            dma((6,)), dma((6,)),
             dma((4, 3)), dma((4, 3)),
             dma((4, 3)), dma((4, 3)),
             dma((4,)), dma((4,)),
@@ -469,7 +481,7 @@
             dma((2, 3)), dma((2, 3)),
             dma, dma,
             dma((2, 4)), dma((2, 4)),
-            dma((2, 3)), dma((2, 3)),
+            dma((2, 3, 4)), dma((2, 3, 4)),
             dma((2, 3)), dma((2, 3)),
         ],
         compiler_params=pltpu.CompilerParams(
@@ -477,6 +489,56 @@
         ),
         cost_estimate=pl.CostEstimate(flops=6 * 10**9, bytes_accessed=8 * 2**20, transcendentals=0),
     )(d, r, at, b, ct)
+
+
+def finish_kernel(
+    left, pivot, diag, solved, xr, pivot_sum, square, solved_out, left_out, pivot_out, diag_out,
+    xr_in, pivot_in, square_in, left_buf, sems,
+):
+    copies = [
+        pltpu.make_async_copy(xr.at[pl.ds(0, 256)], xr_in.at[pl.ds(0, 256)], sems.at[0]),
+        pltpu.make_async_copy(xr.at[pl.ds(256, 256)], xr_in.at[pl.ds(256, 256)], sems.at[1]),
+        pltpu.make_async_copy(pivot_sum, pivot_in, sems.at[2]),
+        pltpu.make_async_copy(square, square_in, sems.at[3]),
+        pltpu.make_async_copy(solved, solved_out, sems.at[4]),
+    ]
+    for copy in copies:
+        copy.start()
+    outward = []
+    for half in range(2):
+        copies[half].wait()
+        cut = pl.ds(half * 256, 256)
+        left_buf[cut] = left[cut] - xr_in[cut]
+        outward.append(pltpu.make_async_copy(left_buf.at[cut], left_out.at[cut], sems.at[5 + half]))
+        outward[half].start()
+    copies[2].wait()
+    copies[3].wait()
+    pivot_out[...] = pivot[...] - pivot_in[...]
+    diag_out[...] = diag[...] - square_in[...]
+    copies[4].wait()
+    for copy in outward:
+        copy.wait()
+
+
+def finish(solved, left, xr, pivot, pivot_sum, diag, square):
+    outs = tuple(jax.ShapeDtypeStruct(a.shape, F32) for a in (solved, left, pivot, diag))
+    in_vmem = pl.BlockSpec(memory_space=pltpu.VMEM)
+    any_space = pl.BlockSpec(memory_space=pl.ANY)
+    return pl.pallas_call(
+        finish_kernel,
+        out_shape=outs,
+        in_specs=[in_vmem] * 3 + [any_space] * 4,
+        out_specs=(any_space, any_space, in_vmem, in_vmem),
+        scratch_shapes=[
+            pltpu.VMEM(xr.shape, F32),
+            pltpu.VMEM(pivot_sum.shape, F32),
+            pltpu.VMEM(square.shape, F32),
+            pltpu.VMEM(left.shape, F32),
+            pltpu.SemaphoreType.DMA((7,)),
+        ],
+        compiler_params=pltpu.CompilerParams(vmem_limit_bytes=60 * 1024 * 1024),
+        cost_estimate=pl.CostEstimate(flops=300000, bytes_accessed=4 * 2**20, transcendentals=0),
+    )(left, pivot, diag, solved, xr, pivot_sum, square)
 
 
 def local(
@@ -489,15 +551,12 @@
     pivot_adjoint,
     diag_adjoint,
 ):
-    rows, width = diag_adjoint.shape
     xr, solved, pivot_sum, square_sum = fused(
         diag_factor, pivot_factor, panel_adjoint.T, left_factor, panel_factor.T
     )
-    global_row = lax.axis_index("row") * rows + lax.broadcasted_iota(jnp.int32, (rows, width), 0)
-    global_col = lax.axis_index("col") * width + lax.broadcasted_iota(jnp.int32, (rows, width), 1)
-    left_out = left_adjoint - xr
-    pivot_out = pivot_adjoint - pivot_sum
-    diag_out = diag_adjoint - jnp.where(global_col <= global_row, square_sum, 0.0)
+    solved, left_out, pivot_out, diag_out = finish(
+        solved, left_adjoint, xr, pivot_adjoint, pivot_sum, diag_adjoint, square_sum
+    )
     return (solved.T, left_out, pivot_out, diag_out)
 
 

time: 94.2 us -> 80.6 us (0.86)
  Pallas kernels: 87.2 us -> 79.8 us
  other arithmetic: 5.32 us -> 0 us
    pallas_call x1, Pallas kernels: 87.2 us -> 72.7 us  [fused(): pl.pallas_call(kernel, out_shape=(jax.ShapeDtypeStruct((512, 512), F32),...]
    pallas_call x0 -> x1, Pallas kernels: none -> 7.04 us  [finish(): pl.pallas_call(finish_kernel, out_shape=outs, in_specs=[in_vmem] * 3 + [a...]
    sub x3 -> x0, other arithmetic: 5.31 us -> none  [the longest x1 2.44 us: local(): left_out = left_adjoint - xr]
where the time goes in v2:
time: 80.6 us; the launch traced here: 80.4 us
  Pallas kernels  79.8 us (99%)
    pallas_call x1, Pallas kernels, fused(): pl.pallas_call(kernel, out_shape=(jax.ShapeDtypeStruct((512, 512), F32),...  72.7 us
    pallas_call x1, Pallas kernels, finish(): pl.pallas_call(finish_kernel, out_shape=outs, in_specs=[in_vmem] * 3 + [a...  7.04 us

profile of v2, /device:TPU:1, one launch (start us, length us, event | category | flops | bytes accessed | tf_op | source)
XLA Modules:
  0.0 80.4 jit_solution(15003410754388043142)
XLA Ops:
  0.6 72.7 %shard_map.111 = (f32[512,512]{1,0:T(8,128)}, f32[64,512]{1,0:T(8,128)}, f32[32,512]{1,0:T(8,128)}, f32[32,64]{1,0:T(8,128)}) custom-call(f32[32,64]{1,0:T(8,128)} %d_ref.1, f32[32,512]{1,0:T(8,128)} %r_ref.1, f32[64,512]{1,0:T(8,128)} %bitcast.3, f32[512,512]{1,0:T(8,128)} %b_ref.1, f32[64,512]{1,0:T(8,128)} %bitcast.4), custom_call_target="tpu_custom_call" | custom-call | flops 6000000000 | bytes 8388608 | tf_op jit(solution)/shard_map/pallas_call | solution.py:433
  73.4 7.0 %shard_map.112 = (f32[64,512]{1,0:T(8,128)}, f32[512,512]{1,0:T(8,128)}, f32[32,512]{1,0:T(8,128)}, f32[32,64]{1,0:T(8,128)}) custom-call(f32[512,512]{1,0:T(8,128)} %left.1, f32[32,512]{1,0:T(8,128)} %pivot.1, f32[32,64]{1,0:T(8,128)} %diag.1, f32[64,512]{1,0:T(8,128)} %get-tuple-element.12.solved, f32[512,512]{1,0:T(8,128)} %get-tuple-element.13.xr, ...), custom_call_target="tpu_custom_call" | custom-call | flops 300000 | bytes 4194304 | tf_op jit(solution)/shard_map/pallas_call | solution.py:527

commit v3 on v2

--- a/solution.py
+++ b/solution.py
@@ -491,54 +491,62 @@
     )(d, r, at, b, ct)
 
 
+QUARTERS = 4
+
+
 def finish_kernel(
-    left, pivot, diag, solved, xr, pivot_sum, square, solved_out, left_out, pivot_out, diag_out,
-    xr_in, pivot_in, square_in, left_buf, sems,
+    solved, left, xr, pivot, pivot_sum, diag, square, solved_out, left_out, pivot_out, diag_out,
+    solved_buf, left_buf, xr_buf, pivot_buf, pivot_in, diag_buf, square_in, in_sems, out_sems,
 ):
-    copies = [
-        pltpu.make_async_copy(xr.at[pl.ds(0, 256)], xr_in.at[pl.ds(0, 256)], sems.at[0]),
-        pltpu.make_async_copy(xr.at[pl.ds(256, 256)], xr_in.at[pl.ds(256, 256)], sems.at[1]),
-        pltpu.make_async_copy(pivot_sum, pivot_in, sems.at[2]),
-        pltpu.make_async_copy(square, square_in, sems.at[3]),
-        pltpu.make_async_copy(solved, solved_out, sems.at[4]),
-    ]
-    for copy in copies:
+    rows = left.shape[0] // QUARTERS
+    cuts = [pl.ds(part * rows, rows) for part in range(QUARTERS)]
+    pairs = []
+    for cut in cuts:
+        pairs += [(left.at[cut], left_buf.at[cut]), (xr.at[cut], xr_buf.at[cut])]
+    pairs += [(solved, solved_buf), (pivot, pivot_buf), (pivot_sum, pivot_in), (diag, diag_buf), (square, square_in)]
+    inward = [pltpu.make_async_copy(src, dst, in_sems.at[i]) for i, (src, dst) in enumerate(pairs)]
+    for copy in inward:
         copy.start()
     outward = []
-    for half in range(2):
-        copies[half].wait()
-        cut = pl.ds(half * 256, 256)
-        left_buf[cut] = left[cut] - xr_in[cut]
-        outward.append(pltpu.make_async_copy(left_buf.at[cut], left_out.at[cut], sems.at[5 + half]))
-        outward[half].start()
-    copies[2].wait()
-    copies[3].wait()
-    pivot_out[...] = pivot[...] - pivot_in[...]
-    diag_out[...] = diag[...] - square_in[...]
-    copies[4].wait()
+
+    def send_out(src, dst):
+        copy = pltpu.make_async_copy(src, dst, out_sems.at[len(outward)])
+        copy.start()
+        outward.append(copy)
+
+    for part, cut in enumerate(cuts):
+        inward[2 * part].wait()
+        inward[2 * part + 1].wait()
+        left_buf[cut] = left_buf[cut] - xr_buf[cut]
+        send_out(left_buf.at[cut], left_out.at[cut])
+    small = inward[2 * QUARTERS:]
+    small[0].wait()
+    send_out(solved_buf, solved_out)
+    small[1].wait()
+    small[2].wait()
+    pivot_buf[...] = pivot_buf[...] - pivot_in[...]
+    send_out(pivot_buf, pivot_out)
+    small[3].wait()
+    small[4].wait()
+    diag_buf[...] = diag_buf[...] - square_in[...]
+    send_out(diag_buf, diag_out)
     for copy in outward:
         copy.wait()
 
 
-def finish(solved, left, xr, pivot, pivot_sum, diag, square):
-    outs = tuple(jax.ShapeDtypeStruct(a.shape, F32) for a in (solved, left, pivot, diag))
-    in_vmem = pl.BlockSpec(memory_space=pltpu.VMEM)
+def finish(*arrays):
+    solved, left, _, pivot, _, diag, _ = arrays
     any_space = pl.BlockSpec(memory_space=pl.ANY)
     return pl.pallas_call(
         finish_kernel,
-        out_shape=outs,
-        in_specs=[in_vmem] * 3 + [any_space] * 4,
-        out_specs=(any_space, any_space, in_vmem, in_vmem),
-        scratch_shapes=[
-            pltpu.VMEM(xr.shape, F32),
-            pltpu.VMEM(pivot_sum.shape, F32),
-            pltpu.VMEM(square.shape, F32),
-            pltpu.VMEM(left.shape, F32),
-            pltpu.SemaphoreType.DMA((7,)),
-        ],
+        out_shape=tuple(jax.ShapeDtypeStruct(a.shape, F32) for a in (solved, left, pivot, diag)),
+        in_specs=[any_space] * 7,
+        out_specs=(any_space,) * 4,
+        scratch_shapes=[pltpu.VMEM(a.shape, F32) for a in arrays]
+        + [pltpu.SemaphoreType.DMA((2 * QUARTERS + 5,)), pltpu.SemaphoreType.DMA((QUARTERS + 3,))],
         compiler_params=pltpu.CompilerParams(vmem_limit_bytes=60 * 1024 * 1024),
         cost_estimate=pl.CostEstimate(flops=300000, bytes_accessed=4 * 2**20, transcendentals=0),
-    )(left, pivot, diag, solved, xr, pivot_sum, square)
+    )(*arrays)
 
 
 def local(

time: 80.6 us -> 76.1 us (0.944)
  Pallas kernels: 79.8 us -> 75.2 us
    pallas_call x1, Pallas kernels: 7.04 us -> 2.47 us  [finish(): pl.pallas_call(finish_kernel, out_shape=tuple((jax.ShapeDtypeStruct(a.sha...]
where the time goes in v3:
time: 76.1 us; the launch traced here: 75.9 us
  Pallas kernels  75.2 us (99%)
    pallas_call x1, Pallas kernels, fused(): pl.pallas_call(kernel, out_shape=(jax.ShapeDtypeStruct((512, 512), F32),...  72.7 us
    pallas_call x1, Pallas kernels, finish(): pl.pallas_call(finish_kernel, out_shape=tuple((jax.ShapeDtypeStruct(a.sha...  2.47 us

profile of v3, /device:TPU:1, one launch (start us, length us, event | category | flops | bytes accessed | tf_op | source)
XLA Modules:
  0.0 75.9 jit_solution(3987120623894803873)
XLA Ops:
  0.6 72.7 %shard_map.111 = (f32[512,512]{1,0:T(8,128)}, f32[64,512]{1,0:T(8,128)}, f32[32,512]{1,0:T(8,128)}, f32[32,64]{1,0:T(8,128)}) custom-call(f32[32,64]{1,0:T(8,128)} %d_ref.1, f32[32,512]{1,0:T(8,128)} %r_ref.1, f32[64,512]{1,0:T(8,128)} %bitcast.3, f32[512,512]{1,0:T(8,128)} %b_ref.1, f32[64,512]{1,0:T(8,128)} %bitcast.4), custom_call_target="tpu_custom_call" | custom-call | flops 6000000000 | bytes 8388608 | tf_op jit(solution)/shard_map/pallas_call | solution.py:433
  73.4 2.5 %shard_map.112 = (f32[64,512]{1,0:T(8,128)}, f32[512,512]{1,0:T(8,128)}, f32[32,512]{1,0:T(8,128)}, f32[32,64]{1,0:T(8,128)}) custom-call(f32[64,512]{1,0:T(8,128)} %get-tuple-element.12.solved, f32[512,512]{1,0:T(8,128)} %left.1, f32[512,512]{1,0:T(8,128)} %get-tuple-element.13.xr, f32[32,512]{1,0:T(8,128)} %pivot.1, ...), custom_call_target="tpu_custom_call" | custom-call | flops 300000 | bytes 4194304 | tf_op jit(solution)/shard_map/pallas_call | solution.py:540
